TPU v7x, 32 devices: a whole 2x2x4 slice. The times are simulated.
32 devices in a mesh: group: 2 (over x), space: 16 (over z, y, core).
Axes of the slice: x: 2, y: 2, z: 4, core: 2. Of those that a mesh axis runs over, the one named last changes fastest.
Arguments:
- snapshots: bfloat16 [32, 3, 256, 128], P('group', None, 'space'), parts along dimension 0, may hold values from -8 to 8
- basis: bfloat16 [128, 3, 128, 256], P('group', None, 'space'), parts along dimension 0, may hold values from -6 to 6
- mode_weights: float32 [128], P('group'), parts along dimension 0, may hold values from 0.5 to 4
- land_mask: int32 [256, 128], P('space'), may hold values 0 or 1
- scale_index: int32 [128], replicated, may hold values from 0 to 15
- scale_values: float32 [16], replicated, may hold values from 0.06 to 0.24
Outputs:
- new_basis: bfloat16 [128, 3, 128, 256], P('group', None, 'space'), parts along dimension 0
- coefficients: float32 [32, 64], P('group'), parts along dimension 0
There are 2 independent parts, one for each index of `group`. A program takes and returns all parts, laid end to end along the dimension named above; an argument that names none is the same for every part. Nothing has to cross between parts.
Inputs may be any that keep to these rules, and one draw needn't show every extreme that they name: `land_mask`: 1 marks ocean, 0 land. Row y uses scale_values[scale_index[y]].
All inputs are finite; a program needn't handle non-finite values. No bound on the sum of `land_mask` on one device may be relied on, other than what follows from the above.
Results may differ from a plain program's by a relative error of at most 0.0057.
Values may be sent and summed in bfloat16 or wider, within the bound.
A program may use at most 128 MiB of HBM per device.

v0:
```python
import math
import jax
import jax.numpy as jnp
from jax import lax
from jax.sharding import PartitionSpec as P

PASS_COEFS = (1.0, 0.95, 0.85, 0.7, 0.5, 0.3)


def with_halo(cells, sides, width):
    for axis, dim in sides:
        count = lax.axis_size(axis)
        head = lax.slice_in_dim(cells, 0, width, axis=dim)
        tail = lax.slice_in_dim(cells, cells.shape[dim] - width, cells.shape[dim], axis=dim)
        cells = jnp.concatenate(
            [
                lax.ppermute(tail, axis, [(i, (i + 1) % count) for i in range(count)]),
                cells,
                lax.ppermute(head, axis, [((i + 1) % count, i) for i in range(count)]),
            ],
            axis=dim,
        )
    return cells


def latitude_scale(scale_index, scale_values):
    levels = jnp.arange(scale_values.shape[0], dtype=jnp.int32)
    matches = (scale_index[None, :] == levels[:, None]).astype(jnp.float32)
    return jnp.sum(matches * scale_values[:, None], axis=0)


def masked_step(fields_now, ocean, factor):
    centre = fields_now[:, :, 1:-1]
    m_centre = ocean[1:-1]
    east_flux = ocean[2:] * (fields_now[:, :, 2:] - centre)
    west_flux = ocean[:-2] * (fields_now[:, :, :-2] - centre)
    padded = jnp.pad(centre, ((0, 0), (0, 0), (0, 0), (1, 1)))
    m_pad = jnp.pad(m_centre, ((0, 0), (1, 1)))
    north_flux = m_pad[:, 2:] * (padded[..., 2:] - centre)
    south_flux = m_pad[:, :-2] * (padded[..., :-2] - centre)
    return centre + factor * (m_centre * (east_flux + west_flux + north_flux + south_flux))


def dot_rows(left, right):
    return lax.dot_general(
        left, right, (((1,), (1,)), ((), ())), preferred_element_type=jnp.float32
    )


def eof_update(data_rows, basis_rows, mode_weights, total_cells):
    high = lax.Precision.HIGHEST
    root_total = math.sqrt(total_cells)
    cross_sum = lax.psum(dot_rows(data_rows, basis_rows), "space")
    coefficients = cross_sum / root_total
    coeff_b = coefficients.astype(jnp.bfloat16)
    update = mode_weights[:, None] * basis_rows.astype(jnp.float32) + lax.dot_general(
        coeff_b, data_rows, (((0,), (0,)), ((), ())), preferred_element_type=jnp.float32
    )
    gram_matrix = lax.psum(jnp.dot(update, update.T, precision=high), "space") / total_cells
    chol_factor = jnp.linalg.cholesky(gram_matrix)
    solved = jax.scipy.linalg.solve_triangular(chol_factor, update, lower=True)
    return (solved.astype(jnp.bfloat16), coefficients)


def local(snapshots, basis, mode_weights, land_mask, scale_index, scale_values):
    lat_scale = latitude_scale(scale_index, scale_values)
    halo_width = 1
    ocean_wide = with_halo(land_mask, (("space", 0),), halo_width).astype(jnp.float32)
    fields_now = snapshots.astype(jnp.float32)
    for group_start in range(0, len(PASS_COEFS), halo_width):
        extended = with_halo(fields_now, (("space", 2),), 1)
        factor = PASS_COEFS[group_start] * lat_scale
        extended = masked_step(extended, ocean_wide, factor)
        fields_now = extended
    ocean = land_mask.astype(jnp.float32)
    filtered = (ocean * fields_now).astype(jnp.bfloat16)
    modes = basis.shape[0]
    snaps = filtered.shape[0]
    slab_data = lax.all_to_all(filtered, "space", split_axis=3, concat_axis=2, tiled=True)
    data_rows = jnp.swapaxes(slab_data, 2, 3).reshape(snaps, -1)
    basis_rows = basis.reshape(modes, -1)
    total_cells = float(data_rows.shape[1] * lax.axis_size("space"))
    solved, coefficients = eof_update(data_rows, basis_rows, mode_weights, total_cells)
    new_basis = solved.reshape(basis.shape)
    return (new_basis, coefficients)


def solution(mesh):
    placed = (
        P("group", None, "space", None),
        P("group", None, "space", None),
        P("group"),
        P("space", None),
        P(),
        P(),
    )
    return jax.shard_map(
        local,
        mesh=mesh,
        in_specs=placed,
        out_specs=(P("group", None, "space", None), P("group", None)),
        check_vma=False,
    )
```

profile of v0, /device:TPU:0, one launch (start us, length us, event | category | flops | bytes accessed | tf_op | source)
XLA Modules:
  0.0 175.6 jit_solution(13503581497344326809)
XLA Ops:
  0.6 0.7 fusion.94
  1.3 0.5 collective-permute-start
  1.8 5.0 %collective-permute-start.1 = (s32[1,128]{1,0:T(1,128)S(1)}, s32[1,128]{1,0:T(1,128)S(1)}, u32[]{:S(2)}, u32[]{:S(2)}) collective-permute-start(s32[1,128]{1,0:T(1,128)S(1)} %get-tuple-element.20), channel_id=1, source_target_pairs={{1,0},{2,1},{3,2},{4,3},{5,4},{6,5},{7,6},{8,7},{9,8},{10,9},{11,1... | collective-permute-start | bytes 1544 | tf_op jit(solution)/shard_map/ppermute | solution.py:19
  6.8 1.0 copy_convert_fusion
  7.8 0.7 collective-permute-start.2
  8.5 0.7 add_convert_fusion
  9.2 0.8 pad_slice_fusion.13
  10.0 4.4 %collective-permute-done.3 = f32[16,3,1,128]{3,0,2,1:T(8,128)S(1)} collective-permute-done((f32[16,3,1,128]{3,0,2,1:T(8,128)S(1)}, f32[16,3,1,128]{3,0,2,1:T(8,128)S(1)}, u32[]{:S(2)}, u32[]{:S(2)}) %collective-permute-start.3) | collective-permute-done | bytes 24608 | tf_op jit(solution)/shard_map/ppermute | solution.py:17
  14.4 1.2 convert_add_fusion
  15.8 0.5 collective-permute-start.5
  16.3 1.0 collective-permute-done.4
  17.3 4.6 %collective-permute-done.5 = f32[16,3,1,128]{3,0,2,1:T(8,128)S(1)} collective-permute-done((f32[16,3,1,128]{3,0,2,1:T(8,128)S(1)}, f32[16,3,1,128]{3,0,2,1:T(8,128)S(1)}, u32[]{:S(2)}, u32[]{:S(2)}) %collective-permute-start.5) | collective-permute-done | bytes 24608 | tf_op jit(solution)/shard_map/ppermute | solution.py:17
  21.8 0.3 fusion.16
  22.2 0.5 collective-permute-start.7
  22.7 1.0 collective-permute-done.6
  23.7 4.5 %collective-permute-done.7 = f32[16,3,1,128]{3,0,2,1:T(8,128)S(1)} collective-permute-done((f32[16,3,1,128]{3,0,2,1:T(8,128)S(1)}, f32[16,3,1,128]{3,0,2,1:T(8,128)S(1)}, u32[]{:S(2)}, u32[]{:S(2)}) %collective-permute-start.7) | collective-permute-done | bytes 24608 | tf_op jit(solution)/shard_map/ppermute | solution.py:17
  28.3 0.3 fusion.25
  28.6 0.5 collective-permute-start.9
  29.1 1.0 collective-permute-done.8
  30.1 4.5 %collective-permute-done.9 = f32[16,3,1,128]{3,0,2,1:T(8,128)S(1)} collective-permute-done((f32[16,3,1,128]{3,0,2,1:T(8,128)S(1)}, f32[16,3,1,128]{3,0,2,1:T(8,128)S(1)}, u32[]{:S(2)}, u32[]{:S(2)}) %collective-permute-start.9) | collective-permute-done | bytes 24608 | tf_op jit(solution)/shard_map/ppermute | solution.py:17
  34.7 0.3 fusion.34
  35.1 0.5 collective-permute-start.11
  35.5 1.0 collective-permute-done.10
  36.6 4.5 %collective-permute-done.11 = f32[16,3,1,128]{3,0,2,1:T(8,128)S(1)} collective-permute-done((f32[16,3,1,128]{3,0,2,1:T(8,128)S(1)}, f32[16,3,1,128]{3,0,2,1:T(8,128)S(1)}, u32[]{:S(2)}, u32[]{:S(2)}) %collective-permute-start.11) | collective-permute-done | bytes 24608 | tf_op jit(solution)/shard_map/ppermute | solution.py:17
  41.1 0.3 fusion.43
  41.5 0.5 collective-permute-start.13
  42.0 1.0 collective-permute-done.12
  43.0 4.5 %collective-permute-done.13 = f32[16,3,1,128]{3,0,2,1:T(8,128)S(1)} collective-permute-done((f32[16,3,1,128]{3,0,2,1:T(8,128)S(1)}, f32[16,3,1,128]{3,0,2,1:T(8,128)S(1)}, u32[]{:S(2)}, u32[]{:S(2)}) %collective-permute-start.13) | collective-permute-done | bytes 24608 | tf_op jit(solution)/shard_map/ppermute | solution.py:17
  47.5 0.3 fusion.54
  47.8 1.1 copy.41
  48.9 2.3 %reshape.52 = bf16[16,2,3072]{2,1,0:T(2,128)(2,1)} reshape(bf16[128,3,16,16]{3,2,1,0:T(8,128)(2,1)S(1)} %bitcast.42) | data formatting | bytes 393216
  51.2 3.5 %all-to-all-start = ((bf16[16,2,3072]{2,1,0:T(2,128)(2,1)}), bf16[16,2,3072]{2,1,0:T(2,128)(2,1)S(1)}, u32[]{:S(2)}, u32[]{:S(2)}) async-start(bf16[16,2,3072]{2,1,0:T(2,128)(2,1)} %reshape.52), calls=%async_computation | async-start | bytes 393216 | tf_op jit(solution)/shard_map/all_to_all | solution.py:79
  54.9 8.8 %all-to-all-done = bf16[16,2,3072]{2,1,0:T(2,128)(2,1)S(1)} async-done(((bf16[16,2,3072]{2,1,0:T(2,128)(2,1)}), bf16[16,2,3072]{2,1,0:T(2,128)(2,1)S(1)}, u32[]{:S(2)}, u32[]{:S(2)}) %all-to-all-start) | async-done | bytes 196640 | tf_op jit(solution)/shard_map/all_to_all | solution.py:79
  63.7 1.2 reshape.53
  64.9 2.2 %copy.43 = bf16[16,3,16,16,8]{3,2,0,4,1:T(8,128)(2,1)} copy(bf16[16,3,16,16,8]{3,0,1,4,2:T(8,128)(2,1)S(1)} %bitcast.43) | data formatting | bytes 393216 | tf_op jit(solution)/shard_map/all_to_all | solution.py:79
  67.1 2.7 %all_to_all.16 = bf16[16,3,256,8]{2,0,3,1:T(8,128)(2,1)S(1)} reshape(bf16[16,3,16,16,8]{3,2,0,4,1:T(8,128)(2,1)} %copy.43) | data formatting | bytes 393216 | tf_op jit(solution)/shard_map/all_to_all | solution.py:79
  69.8 0.3 convolution_bitcast_fusion
  70.1 31.0 %psum.14 = f32[16,64]{1,0:T(8,128)S(1)} all-reduce(f32[16,64]{1,0:T(8,128)S(1)} %convolution_bitcast_fusion), channel_id=1, replica_groups=mesh['group'=2,'space'=16] {'space'}, use_global_device_ids=true, to_apply=%region_1.2 | all-reduce | flops 1024 | bytes 8192 | tf_op jit(solution)/shard_map/psum | solution.py:53
  101.1 0.4 convolution_add_fusion
  101.5 0.2 copy-done.3
  101.7 1.4 fusion.95
  103.1 57.8 %psum.15 = f32[64,64]{0,1:T(8,128)S(1)} all-reduce(f32[64,64]{0,1:T(8,128)S(1)} %fusion.95), channel_id=1, replica_groups=mesh['group'=2,'space'=16] {'space'}, use_global_device_ids=true, to_apply=%region_2.3 | all-reduce | flops 4096 | bytes 32768 | tf_op jit(solution)/shard_map/psum | solution.py:59
  161.0 5.8 %cholesky.16 = f32[64,64]{1,0:T(8,128)S(1)} custom-call(f32[64,64]{1,0:T(8,128)S(1)} %fusion.84), custom_call_target="Cholesky" | custom-call | tf_op jit(solution)/shard_map/jit(cholesky)/cholesky | solution.py:60
  166.9 0.6 compare_reduce_fusion
  167.5 0.7 fusion.82
  168.2 4.9 %custom-call.7 = f32[1,64,64]{1,2,0:T(8,128)S(1)} custom-call(f32[1,64,64]{2,1,0:T(8,128)S(1)} %fusion.82), custom_call_target="InvertDiagBlocksLowerTriangular" | custom-call | tf_op jit(solution)/shard_map/jit(_solve_triangular)/triangular_solve | solution.py:61
  173.1 1.5 convolution_convert_fusion
  174.6 1.0 copy.53
  (34 shorter events, 0.7 us)
Async XLA Ops:
  1.3 7.2 %collective-permute-start = (s32[1,128]{1,0:T(1,128)S(1)}, s32[1,128]{1,0:T(1,128)S(1)}, u32[]{:S(2)}, u32[]{:S(2)}) collective-permute-start(s32[1,128]{1,0:T(1,128)S(1)} %get-tuple-element.19), channel_id=1, source_target_pairs={{0,1},{1,2},{2,3},{3,4},{4,5},{5,6},{6,7},{7,8},{8,9},{9,10},{10,1... | collective-permute-start | bytes 1544 | tf_op jit(solution)/shard_map/ppermute | solution.py:17
  1.8 6.7 %collective-permute-start.1 = (s32[1,128]{1,0:T(1,128)S(1)}, s32[1,128]{1,0:T(1,128)S(1)}, u32[]{:S(2)}, u32[]{:S(2)}) collective-permute-start(s32[1,128]{1,0:T(1,128)S(1)} %get-tuple-element.20), channel_id=1, source_target_pairs={{1,0},{2,1},{3,2},{4,3},{5,4},{6,5},{7,6},{8,7},{9,8},{10,9},{11,1... | collective-permute-start | bytes 1544 | tf_op jit(solution)/shard_map/ppermute | solution.py:19
  7.8 2.2 %collective-permute-start.2 = (f32[16,3,1,128]{3,0,2,1:T(8,128)S(1)}, f32[16,3,1,128]{3,0,2,1:T(8,128)S(1)}, u32[]{:S(2)}, u32[]{:S(2)}) collective-permute-start(f32[16,3,1,128]{3,0,2,1:T(8,128)S(1)} %get-tuple-element.12), channel_id=1, source_target_pairs={{1,0},{2,1},{3,2},{4,3},{5,4},{6,5},{7,6},{8,7},{9,8},{10,9},{11,1... | collective-permute-start | bytes 73736 | tf_op jit(solution)/shard_map/ppermute | solution.py:19
  8.5 5.9 %collective-permute-start.3 = (f32[16,3,1,128]{3,0,2,1:T(8,128)S(1)}, f32[16,3,1,128]{3,0,2,1:T(8,128)S(1)}, u32[]{:S(2)}, u32[]{:S(2)}) collective-permute-start(f32[16,3,1,128]{3,0,2,1:T(8,128)S(1)} %get-tuple-element.13), channel_id=1, source_target_pairs={{0,1},{1,2},{2,3},{3,4},{4,5},{5,6},{6,7},{7,8},{8,9},{9,10},{10,1... | collective-permute-start | bytes 73736 | tf_op jit(solution)/shard_map/ppermute | solution.py:17
  15.7 1.6 collective-permute-start.4
  15.8 6.1 %collective-permute-start.5 = (f32[16,3,1,128]{3,0,2,1:T(8,128)S(1)}, f32[16,3,1,128]{3,0,2,1:T(8,128)S(1)}, u32[]{:S(2)}, u32[]{:S(2)}) collective-permute-start(f32[16,3,1,128]{3,0,2,1:T(8,128)S(1)} %get-tuple-element.11), channel_id=1, source_target_pairs={{0,1},{1,2},{2,3},{3,4},{4,5},{5,6},{6,7},{7,8},{8,9},{9,10},{10,1... | collective-permute-start | bytes 73736 | tf_op jit(solution)/shard_map/ppermute | solution.py:17
  22.1 19.9 %copy-start.2 = (s32[16,128]{1,0:T(8,128)S(1)}, s32[16,128]{1,0:T(8,128)}, u32[]{:S(2)}) copy-start(s32[16,128]{1,0:T(8,128)} %param.9) | copy-start | bytes 24580
  22.1 1.6 collective-permute-start.6
  22.2 6.1 %collective-permute-start.7 = (f32[16,3,1,128]{3,0,2,1:T(8,128)S(1)}, f32[16,3,1,128]{3,0,2,1:T(8,128)S(1)}, u32[]{:S(2)}, u32[]{:S(2)}) collective-permute-start(f32[16,3,1,128]{3,0,2,1:T(8,128)S(1)} %get-tuple-element.9), channel_id=1, source_target_pairs={{0,1},{1,2},{2,3},{3,4},{4,5},{5,6},{6,7},{7,8},{8,9},{9,10},{10,1... | collective-permute-start | bytes 73736 | tf_op jit(solution)/shard_map/ppermute | solution.py:17
  28.6 1.6 collective-permute-start.8
  28.6 6.1 %collective-permute-start.9 = (f32[16,3,1,128]{3,0,2,1:T(8,128)S(1)}, f32[16,3,1,128]{3,0,2,1:T(8,128)S(1)}, u32[]{:S(2)}, u32[]{:S(2)}) collective-permute-start(f32[16,3,1,128]{3,0,2,1:T(8,128)S(1)} %get-tuple-element.7), channel_id=1, source_target_pairs={{0,1},{1,2},{2,3},{3,4},{4,5},{5,6},{6,7},{7,8},{8,9},{9,10},{10,1... | collective-permute-start | bytes 73736 | tf_op jit(solution)/shard_map/ppermute | solution.py:17
  35.0 1.6 collective-permute-start.10
  35.1 6.1 %collective-permute-start.11 = (f32[16,3,1,128]{3,0,2,1:T(8,128)S(1)}, f32[16,3,1,128]{3,0,2,1:T(8,128)S(1)}, u32[]{:S(2)}, u32[]{:S(2)}) collective-permute-start(f32[16,3,1,128]{3,0,2,1:T(8,128)S(1)} %get-tuple-element.5), channel_id=1, source_target_pairs={{0,1},{1,2},{2,3},{3,4},{4,5},{5,6},{6,7},{7,8},{8,9},{9,10},{10,1... | collective-permute-start | bytes 73736 | tf_op jit(solution)/shard_map/ppermute | solution.py:17
  41.4 1.6 collective-permute-start.12
  41.5 6.0 %collective-permute-start.13 = (f32[16,3,1,128]{3,0,2,1:T(8,128)S(1)}, f32[16,3,1,128]{3,0,2,1:T(8,128)S(1)}, u32[]{:S(2)}, u32[]{:S(2)}) collective-permute-start(f32[16,3,1,128]{3,0,2,1:T(8,128)S(1)} %get-tuple-element.3), channel_id=1, source_target_pairs={{0,1},{1,2},{2,3},{3,4},{4,5},{5,6},{6,7},{7,8},{8,9},{9,10},{10,1... | collective-permute-start | bytes 73736 | tf_op jit(solution)/shard_map/ppermute | solution.py:17
  47.8 7.0 %copy-start = (bf16[64,3,8,256]{3,2,1,0:T(8,128)(2,1)S(1)}, bf16[64,3,8,256]{3,2,1,0:T(8,128)(2,1)}, u32[]{:S(2)}) copy-start(bf16[64,3,8,256]{3,2,1,0:T(8,128)(2,1)} %param.7) | copy-start | bytes 2359300
  51.2 12.5 %all-to-all-start = ((bf16[16,2,3072]{2,1,0:T(2,128)(2,1)}), bf16[16,2,3072]{2,1,0:T(2,128)(2,1)S(1)}, u32[]{:S(2)}, u32[]{:S(2)}) async-start(bf16[16,2,3072]{2,1,0:T(2,128)(2,1)} %reshape.52), calls=%async_computation | async-start | bytes 393216 | tf_op jit(solution)/shard_map/all_to_all | solution.py:79
  67.1 2.7 %copy-start.1 = (bf16[64,3,8,256]{3,2,1,0:T(8,128)(2,1)S(1)}, bf16[64,3,8,256]{3,2,1,0:T(8,128)(2,1)}, u32[]{:S(2)}) copy-start(bf16[64,3,8,256]{3,2,1,0:T(8,128)(2,1)} %param.7) | copy-start | bytes 2359300
  67.1 34.0 %copy-start.4 = (f32[64]{0:T(128)S(1)}, f32[64]{0:T(128)}, u32[]{:S(2)}) copy-start(f32[64]{0:T(128)} %param.8) | copy-start | bytes 772
  101.1 0.6 copy-start.3
where the time goes:
time: 176 us
  blocking collectives  88.8 us (50%)
  waiting for transfers between devices  41 us (23%)
  other arithmetic  17.2 us (10%)
  starting transfers between devices  12.5 us (7%)
  local copies, waits for them, and re-layouts  11.7 us (7%)
  matrix products  3.56 us (2%)
    psum x1, blocking collectives, eof_update(): lax.psum(jnp.dot(update, update.T, precision=high), 'space') / total_cells  57.8 us
    psum x1, blocking collectives, eof_update(): cross_sum = lax.psum(dot_rows(data_rows, basis_rows), 'space')  31 us
    ppermute x7, waiting for transfers between devices, with_halo(): lax.ppermute(tail, axis, [(i, (i + 1) % count) for i in range(count)])  27.1 us
    all_to_all x1, waiting for transfers between devices, local(): lax.all_to_all(filtered, 'space', split_axis=3, concat_axis=2, tiled=True)  8.79 us
    another operation x3, other arithmetic, eof_update(): chol_factor = jnp.linalg.cholesky(gram_matrix)  6.52 us
    ppermute x7, starting transfers between devices, with_halo(): lax.ppermute(head, axis, [((i + 1) % count, i) for i in range(count)])  6.01 us
    another operation x2, other arithmetic, eof_update(): solved = jax.scipy.linalg.solve_triangular(chol_factor, update, lower=True)  5.55 us
    ppermute x7, waiting for transfers between devices, with_halo(): lax.ppermute(head, axis, [((i + 1) % count, i) for i in range(count)])  5.11 us
  transfers between devices with their start and end apart: 15, of which 12 were waited for; matrix products, arithmetic and copies ran while one was open for 1% of the time, Pallas kernels for 0%

commit v1 on v0

--- a/solution.py
+++ b/solution.py
@@ -1,3 +1,4 @@
+import functools
 import math
 import jax
 import jax.numpy as jnp
@@ -5,6 +6,14 @@
 from jax.sharding import PartitionSpec as P
 
 PASS_COEFS = (1.0, 0.95, 0.85, 0.7, 0.5, 0.3)
+
+
+def produce_core_by_axis(array_here, named_axis):
+    block_out = lax.all_gather(array_here, axis_name=named_axis)
+    return jnp.sum(block_out, axis=0)
+
+
+boxes_make = functools.partial(produce_core_by_axis, named_axis="space")
 
 
 def with_halo(cells, sides, width):
@@ -56,7 +65,7 @@
     update = mode_weights[:, None] * basis_rows.astype(jnp.float32) + lax.dot_general(
         coeff_b, data_rows, (((0,), (0,)), ((), ())), preferred_element_type=jnp.float32
     )
-    gram_matrix = lax.psum(jnp.dot(update, update.T, precision=high), "space") / total_cells
+    gram_matrix = boxes_make(jnp.dot(update, update.T, precision=high)) / total_cells
     chol_factor = jnp.linalg.cholesky(gram_matrix)
     solved = jax.scipy.linalg.solve_triangular(chol_factor, update, lower=True)
     return (solved.astype(jnp.bfloat16), coefficients)

time: 176 us -> 137 us (0.78)
  blocking collectives: 88.8 us -> 50 us
    psum x1 -> x0, blocking collectives: 57.8 us -> none  [eof_update(): lax.psum(jnp.dot(update, update.T, precision=high), 'space') / total_cells]
    all_gather x0 -> x1, blocking collectives: none -> 19 us  [produce_core_by_axis(): block_out = lax.all_gather(array_here, axis_name=named_axis)]
    unnamed x15 -> x13, local copies, waits for them, and re-layouts: 4.89 us -> 6.02 us
  transfers between devices with their start and end apart: 15 -> 15, of which waited for: 12 -> 12; matrix products, arithmetic and copies ran while one was open for 1% -> 3% of each run, Pallas kernels for 0% -> 0%
where the time goes in v1:
time: 137 us
  blocking collectives  50 us (36%)
  waiting for transfers between devices  39.9 us (29%)
  other arithmetic  17.2 us (13%)
  local copies, waits for them, and re-layouts  12.9 us (9%)
  starting transfers between devices  12.5 us (9%)
  matrix products  3.56 us (3%)
    psum x1, blocking collectives, eof_update(): cross_sum = lax.psum(dot_rows(data_rows, basis_rows), 'space')  31 us
    ppermute x7, waiting for transfers between devices, with_halo(): lax.ppermute(tail, axis, [(i, (i + 1) % count) for i in range(count)])  27.1 us
    all_gather x1, blocking collectives, produce_core_by_axis(): block_out = lax.all_gather(array_here, axis_name=named_axis)  19 us
    all_to_all x1, waiting for transfers between devices, local(): lax.all_to_all(filtered, 'space', split_axis=3, concat_axis=2, tiled=True)  7.67 us
    another operation x3, other arithmetic, eof_update(): chol_factor = jnp.linalg.cholesky(gram_matrix)  6.52 us
    unnamed x13, local copies, waits for them, and re-layouts  6.02 us
    ppermute x7, starting transfers between devices, with_halo(): lax.ppermute(head, axis, [((i + 1) % count, i) for i in range(count)])  6.01 us
    another operation x2, other arithmetic, eof_update(): solved = jax.scipy.linalg.solve_triangular(chol_factor, update, lower=True)  5.55 us
  transfers between devices with their start and end apart: 15, of which 12 were waited for; matrix products, arithmetic and copies ran while one was open for 3% of the time, Pallas kernels for 0%

profile of v1, /device:TPU:0, one launch (start us, length us, event | category | flops | bytes accessed | tf_op | source)
XLA Modules:
  0.0 136.9 jit_solution(10889309395529327780)
XLA Ops:
  0.6 0.7 fusion.94
  1.3 0.5 collective-permute-start
  1.8 5.0 %collective-permute-start.1 = (s32[1,128]{1,0:T(1,128)S(1)}, s32[1,128]{1,0:T(1,128)S(1)}, u32[]{:S(2)}, u32[]{:S(2)}) collective-permute-start(s32[1,128]{1,0:T(1,128)S(1)} %get-tuple-element.20), channel_id=1, source_target_pairs={{1,0},{2,1},{3,2},{4,3},{5,4},{6,5},{7,6},{8,7},{9,8},{10,9},{11,1... | collective-permute-start | bytes 1544 | tf_op jit(solution)/shard_map/ppermute | solution.py:28
  6.8 1.0 copy_convert_fusion
  7.8 0.7 collective-permute-start.2
  8.5 0.7 add_convert_fusion
  9.2 0.8 pad_slice_fusion.13
  10.0 4.4 %collective-permute-done.3 = f32[16,3,1,128]{3,0,2,1:T(8,128)S(1)} collective-permute-done((f32[16,3,1,128]{3,0,2,1:T(8,128)S(1)}, f32[16,3,1,128]{3,0,2,1:T(8,128)S(1)}, u32[]{:S(2)}, u32[]{:S(2)}) %collective-permute-start.3) | collective-permute-done | bytes 24608 | tf_op jit(solution)/shard_map/ppermute | solution.py:26
  14.4 1.2 convert_add_fusion
  15.8 0.5 collective-permute-start.5
  16.3 1.0 collective-permute-done.4
  17.3 4.6 %collective-permute-done.5 = f32[16,3,1,128]{3,0,2,1:T(8,128)S(1)} collective-permute-done((f32[16,3,1,128]{3,0,2,1:T(8,128)S(1)}, f32[16,3,1,128]{3,0,2,1:T(8,128)S(1)}, u32[]{:S(2)}, u32[]{:S(2)}) %collective-permute-start.5) | collective-permute-done | bytes 24608 | tf_op jit(solution)/shard_map/ppermute | solution.py:26
  21.8 0.3 fusion.16
  22.2 0.5 collective-permute-start.7
  22.7 1.0 collective-permute-done.6
  23.7 4.5 %collective-permute-done.7 = f32[16,3,1,128]{3,0,2,1:T(8,128)S(1)} collective-permute-done((f32[16,3,1,128]{3,0,2,1:T(8,128)S(1)}, f32[16,3,1,128]{3,0,2,1:T(8,128)S(1)}, u32[]{:S(2)}, u32[]{:S(2)}) %collective-permute-start.7) | collective-permute-done | bytes 24608 | tf_op jit(solution)/shard_map/ppermute | solution.py:26
  28.3 0.3 fusion.25
  28.6 0.5 collective-permute-start.9
  29.1 1.0 collective-permute-done.8
  30.1 4.5 %collective-permute-done.9 = f32[16,3,1,128]{3,0,2,1:T(8,128)S(1)} collective-permute-done((f32[16,3,1,128]{3,0,2,1:T(8,128)S(1)}, f32[16,3,1,128]{3,0,2,1:T(8,128)S(1)}, u32[]{:S(2)}, u32[]{:S(2)}) %collective-permute-start.9) | collective-permute-done | bytes 24608 | tf_op jit(solution)/shard_map/ppermute | solution.py:26
  34.7 0.3 fusion.34
  35.1 0.5 collective-permute-start.11
  35.5 1.0 collective-permute-done.10
  36.6 4.5 %collective-permute-done.11 = f32[16,3,1,128]{3,0,2,1:T(8,128)S(1)} collective-permute-done((f32[16,3,1,128]{3,0,2,1:T(8,128)S(1)}, f32[16,3,1,128]{3,0,2,1:T(8,128)S(1)}, u32[]{:S(2)}, u32[]{:S(2)}) %collective-permute-start.11) | collective-permute-done | bytes 24608 | tf_op jit(solution)/shard_map/ppermute | solution.py:26
  41.1 0.3 fusion.43
  41.5 0.5 collective-permute-start.13
  42.0 1.0 collective-permute-done.12
  43.0 4.5 %collective-permute-done.13 = f32[16,3,1,128]{3,0,2,1:T(8,128)S(1)} collective-permute-done((f32[16,3,1,128]{3,0,2,1:T(8,128)S(1)}, f32[16,3,1,128]{3,0,2,1:T(8,128)S(1)}, u32[]{:S(2)}, u32[]{:S(2)}) %collective-permute-start.13) | collective-permute-done | bytes 24608 | tf_op jit(solution)/shard_map/ppermute | solution.py:26
  47.5 0.3 fusion.54
  47.8 1.1 copy.39
  48.9 2.3 %reshape.53 = bf16[16,2,3072]{2,1,0:T(2,128)(2,1)} reshape(bf16[128,3,16,16]{3,2,1,0:T(8,128)(2,1)S(1)} %bitcast.43) | data formatting | bytes 393216
  51.2 3.5 %all-to-all-start = ((bf16[16,2,3072]{2,1,0:T(2,128)(2,1)}), bf16[16,2,3072]{2,1,0:T(2,128)(2,1)S(1)}, u32[]{:S(2)}, u32[]{:S(2)}) async-start(bf16[16,2,3072]{2,1,0:T(2,128)(2,1)} %reshape.53), calls=%async_computation | async-start | bytes 393216 | tf_op jit(solution)/shard_map/all_to_all | solution.py:88
  54.8 1.3 copy.48
  56.1 7.7 %all-to-all-done = bf16[16,2,3072]{2,1,0:T(2,128)(2,1)S(1)} async-done(((bf16[16,2,3072]{2,1,0:T(2,128)(2,1)}), bf16[16,2,3072]{2,1,0:T(2,128)(2,1)S(1)}, u32[]{:S(2)}, u32[]{:S(2)}) %all-to-all-start) | async-done | bytes 196640 | tf_op jit(solution)/shard_map/all_to_all | solution.py:88
  63.7 1.2 reshape.54
  64.9 2.2 %copy.41 = bf16[16,3,16,16,8]{3,2,0,4,1:T(8,128)(2,1)} copy(bf16[16,3,16,16,8]{3,0,1,4,2:T(8,128)(2,1)S(1)} %bitcast.44) | data formatting | bytes 393216 | tf_op jit(solution)/shard_map/all_to_all | solution.py:88
  67.1 2.7 %all_to_all.16 = bf16[16,3,256,8]{2,0,3,1:T(8,128)(2,1)S(1)} reshape(bf16[16,3,16,16,8]{3,2,0,4,1:T(8,128)(2,1)} %copy.41) | data formatting | bytes 393216 | tf_op jit(solution)/shard_map/all_to_all | solution.py:88
  69.8 0.3 convolution_bitcast_fusion
  70.1 31.0 %psum.7 = f32[16,64]{1,0:T(8,128)S(1)} all-reduce(f32[16,64]{1,0:T(8,128)S(1)} %convolution_bitcast_fusion), channel_id=1, replica_groups=mesh['group'=2,'space'=16] {'space'}, use_global_device_ids=true, to_apply=%region_1.2 | all-reduce | flops 1024 | bytes 8192 | tf_op jit(solution)/shard_map/psum | solution.py:62
  101.1 0.4 convolution_add_fusion
  101.7 1.4 %fusion.95 = f32[64,64]{1,0:T(8,128)S(1)} fusion(f32[64,6144]{1,0:T(8,128)S(1)} %convolution_add_fusion), kind=kOutput, calls=%fused_computation.146 | convolution fusion | flops 301989888 | bytes 1589248 | tf_op jit(solution)/shard_map/dot_general | solution.py:68
  103.0 19.0 %all-gather = f32[1024,64]{1,0:T(8,128)S(1)} all-gather(f32[64,64]{1,0:T(8,128)S(1)} %fusion.95), channel_id=2, replica_groups=mesh['group'=2,'space'=16] {'space'}, dimensions={0}, use_global_device_ids=true | all-gather | bytes 278528 | tf_op jit(solution)/shard_map/all_gather | solution.py:12
  122.3 5.8 %cholesky.16 = f32[64,64]{1,0:T(8,128)S(1)} custom-call(f32[64,64]{1,0:T(8,128)S(1)} %fusion.84), custom_call_target="Cholesky" | custom-call | tf_op jit(solution)/shard_map/jit(cholesky)/cholesky | solution.py:69
  128.2 0.6 compare_reduce_fusion
  128.8 0.7 fusion.82
  129.5 4.9 %custom-call.7 = f32[1,64,64]{1,2,0:T(8,128)S(1)} custom-call(f32[1,64,64]{2,1,0:T(8,128)S(1)} %fusion.82), custom_call_target="InvertDiagBlocksLowerTriangular" | custom-call | tf_op jit(solution)/shard_map/jit(_solve_triangular)/triangular_solve | solution.py:70
  134.4 1.5 %convolution_convert_fusion = bf16[64,6144]{1,0:T(8,128)(2,1)S(1)} fusion(f32[64,6144]{1,0:T(8,128)S(1)} %convolution_add_fusion, f32[1,64,64]{1,2,0:T(8,128)S(1)} %custom-call.7), kind=kOutput, calls=%fused_computation.1 | convolution fusion | flops 302383104 | bytes 2375680 | tf_op jit(solution)/shard_map/jit(_solve_triangular)/triangular_solve | solution.py:70
  135.8 1.0 copy.50
  (34 shorter events, 0.8 us)
Async XLA Ops:
  1.3 7.2 %collective-permute-start = (s32[1,128]{1,0:T(1,128)S(1)}, s32[1,128]{1,0:T(1,128)S(1)}, u32[]{:S(2)}, u32[]{:S(2)}) collective-permute-start(s32[1,128]{1,0:T(1,128)S(1)} %get-tuple-element.19), channel_id=1, source_target_pairs={{0,1},{1,2},{2,3},{3,4},{4,5},{5,6},{6,7},{7,8},{8,9},{9,10},{10,1... | collective-permute-start | bytes 1544 | tf_op jit(solution)/shard_map/ppermute | solution.py:26
  1.8 6.7 %collective-permute-start.1 = (s32[1,128]{1,0:T(1,128)S(1)}, s32[1,128]{1,0:T(1,128)S(1)}, u32[]{:S(2)}, u32[]{:S(2)}) collective-permute-start(s32[1,128]{1,0:T(1,128)S(1)} %get-tuple-element.20), channel_id=1, source_target_pairs={{1,0},{2,1},{3,2},{4,3},{5,4},{6,5},{7,6},{8,7},{9,8},{10,9},{11,1... | collective-permute-start | bytes 1544 | tf_op jit(solution)/shard_map/ppermute | solution.py:28
  7.8 2.2 %collective-permute-start.2 = (f32[16,3,1,128]{3,0,2,1:T(8,128)S(1)}, f32[16,3,1,128]{3,0,2,1:T(8,128)S(1)}, u32[]{:S(2)}, u32[]{:S(2)}) collective-permute-start(f32[16,3,1,128]{3,0,2,1:T(8,128)S(1)} %get-tuple-element.12), channel_id=1, source_target_pairs={{1,0},{2,1},{3,2},{4,3},{5,4},{6,5},{7,6},{8,7},{9,8},{10,9},{11,1... | collective-permute-start | bytes 73736 | tf_op jit(solution)/shard_map/ppermute | solution.py:28
  8.5 5.9 %collective-permute-start.3 = (f32[16,3,1,128]{3,0,2,1:T(8,128)S(1)}, f32[16,3,1,128]{3,0,2,1:T(8,128)S(1)}, u32[]{:S(2)}, u32[]{:S(2)}) collective-permute-start(f32[16,3,1,128]{3,0,2,1:T(8,128)S(1)} %get-tuple-element.13), channel_id=1, source_target_pairs={{0,1},{1,2},{2,3},{3,4},{4,5},{5,6},{6,7},{7,8},{8,9},{9,10},{10,1... | collective-permute-start | bytes 73736 | tf_op jit(solution)/shard_map/ppermute | solution.py:26
  15.7 1.6 %collective-permute-start.4 = (f32[16,3,1,128]{3,0,2,1:T(8,128)S(1)}, f32[16,3,1,128]{3,0,2,1:T(8,128)S(1)}, u32[]{:S(2)}, u32[]{:S(2)}) collective-permute-start(f32[16,3,1,128]{3,0,2,1:T(8,128)S(1)} %get-tuple-element.10), channel_id=1, source_target_pairs={{1,0},{2,1},{3,2},{4,3},{5,4},{6,5},{7,6},{8,7},{9,8},{10,9},{11,1... | collective-permute-start | bytes 73736 | tf_op jit(solution)/shard_map/ppermute | solution.py:28
  15.8 6.1 %collective-permute-start.5 = (f32[16,3,1,128]{3,0,2,1:T(8,128)S(1)}, f32[16,3,1,128]{3,0,2,1:T(8,128)S(1)}, u32[]{:S(2)}, u32[]{:S(2)}) collective-permute-start(f32[16,3,1,128]{3,0,2,1:T(8,128)S(1)} %get-tuple-element.11), channel_id=1, source_target_pairs={{0,1},{1,2},{2,3},{3,4},{4,5},{5,6},{6,7},{7,8},{8,9},{9,10},{10,1... | collective-permute-start | bytes 73736 | tf_op jit(solution)/shard_map/ppermute | solution.py:26
  22.1 19.9 %copy-start.1 = (s32[16,128]{1,0:T(8,128)S(1)}, s32[16,128]{1,0:T(8,128)}, u32[]{:S(2)}) copy-start(s32[16,128]{1,0:T(8,128)} %param.9) | copy-start | bytes 24580
  22.1 1.6 %collective-permute-start.6 = (f32[16,3,1,128]{3,0,2,1:T(8,128)S(1)}, f32[16,3,1,128]{3,0,2,1:T(8,128)S(1)}, u32[]{:S(2)}, u32[]{:S(2)}) collective-permute-start(f32[16,3,1,128]{3,0,2,1:T(8,128)S(1)} %get-tuple-element.8), channel_id=1, source_target_pairs={{1,0},{2,1},{3,2},{4,3},{5,4},{6,5},{7,6},{8,7},{9,8},{10,9},{11,1... | collective-permute-start | bytes 73736 | tf_op jit(solution)/shard_map/ppermute | solution.py:28
  22.2 6.1 %collective-permute-start.7 = (f32[16,3,1,128]{3,0,2,1:T(8,128)S(1)}, f32[16,3,1,128]{3,0,2,1:T(8,128)S(1)}, u32[]{:S(2)}, u32[]{:S(2)}) collective-permute-start(f32[16,3,1,128]{3,0,2,1:T(8,128)S(1)} %get-tuple-element.9), channel_id=1, source_target_pairs={{0,1},{1,2},{2,3},{3,4},{4,5},{5,6},{6,7},{7,8},{8,9},{9,10},{10,1... | collective-permute-start | bytes 73736 | tf_op jit(solution)/shard_map/ppermute | solution.py:26
  28.6 1.6 %collective-permute-start.8 = (f32[16,3,1,128]{3,0,2,1:T(8,128)S(1)}, f32[16,3,1,128]{3,0,2,1:T(8,128)S(1)}, u32[]{:S(2)}, u32[]{:S(2)}) collective-permute-start(f32[16,3,1,128]{3,0,2,1:T(8,128)S(1)} %get-tuple-element.6), channel_id=1, source_target_pairs={{1,0},{2,1},{3,2},{4,3},{5,4},{6,5},{7,6},{8,7},{9,8},{10,9},{11,1... | collective-permute-start | bytes 73736 | tf_op jit(solution)/shard_map/ppermute | solution.py:28
  28.6 6.1 %collective-permute-start.9 = (f32[16,3,1,128]{3,0,2,1:T(8,128)S(1)}, f32[16,3,1,128]{3,0,2,1:T(8,128)S(1)}, u32[]{:S(2)}, u32[]{:S(2)}) collective-permute-start(f32[16,3,1,128]{3,0,2,1:T(8,128)S(1)} %get-tuple-element.7), channel_id=1, source_target_pairs={{0,1},{1,2},{2,3},{3,4},{4,5},{5,6},{6,7},{7,8},{8,9},{9,10},{10,1... | collective-permute-start | bytes 73736 | tf_op jit(solution)/shard_map/ppermute | solution.py:26
  35.0 1.6 %collective-permute-start.10 = (f32[16,3,1,128]{3,0,2,1:T(8,128)S(1)}, f32[16,3,1,128]{3,0,2,1:T(8,128)S(1)}, u32[]{:S(2)}, u32[]{:S(2)}) collective-permute-start(f32[16,3,1,128]{3,0,2,1:T(8,128)S(1)} %get-tuple-element.4), channel_id=1, source_target_pairs={{1,0},{2,1},{3,2},{4,3},{5,4},{6,5},{7,6},{8,7},{9,8},{10,9},{11,1... | collective-permute-start | bytes 73736 | tf_op jit(solution)/shard_map/ppermute | solution.py:28
  35.1 6.1 %collective-permute-start.11 = (f32[16,3,1,128]{3,0,2,1:T(8,128)S(1)}, f32[16,3,1,128]{3,0,2,1:T(8,128)S(1)}, u32[]{:S(2)}, u32[]{:S(2)}) collective-permute-start(f32[16,3,1,128]{3,0,2,1:T(8,128)S(1)} %get-tuple-element.5), channel_id=1, source_target_pairs={{0,1},{1,2},{2,3},{3,4},{4,5},{5,6},{6,7},{7,8},{8,9},{9,10},{10,1... | collective-permute-start | bytes 73736 | tf_op jit(solution)/shard_map/ppermute | solution.py:26
  41.4 1.6 %collective-permute-start.12 = (f32[16,3,1,128]{3,0,2,1:T(8,128)S(1)}, f32[16,3,1,128]{3,0,2,1:T(8,128)S(1)}, u32[]{:S(2)}, u32[]{:S(2)}) collective-permute-start(f32[16,3,1,128]{3,0,2,1:T(8,128)S(1)} %get-tuple-element.2), channel_id=1, source_target_pairs={{1,0},{2,1},{3,2},{4,3},{5,4},{6,5},{7,6},{8,7},{9,8},{10,9},{11,1... | collective-permute-start | bytes 73736 | tf_op jit(solution)/shard_map/ppermute | solution.py:28
  41.5 6.0 %collective-permute-start.13 = (f32[16,3,1,128]{3,0,2,1:T(8,128)S(1)}, f32[16,3,1,128]{3,0,2,1:T(8,128)S(1)}, u32[]{:S(2)}, u32[]{:S(2)}) collective-permute-start(f32[16,3,1,128]{3,0,2,1:T(8,128)S(1)} %get-tuple-element.3), channel_id=1, source_target_pairs={{0,1},{1,2},{2,3},{3,4},{4,5},{5,6},{6,7},{7,8},{8,9},{9,10},{10,1... | collective-permute-start | bytes 73736 | tf_op jit(solution)/shard_map/ppermute | solution.py:26
  51.2 12.5 %all-to-all-start = ((bf16[16,2,3072]{2,1,0:T(2,128)(2,1)}), bf16[16,2,3072]{2,1,0:T(2,128)(2,1)S(1)}, u32[]{:S(2)}, u32[]{:S(2)}) async-start(bf16[16,2,3072]{2,1,0:T(2,128)(2,1)} %reshape.53), calls=%async_computation | async-start | bytes 393216 | tf_op jit(solution)/shard_map/all_to_all | solution.py:88
  67.1 2.7 %copy-start = (bf16[64,3,8,256]{3,2,1,0:T(8,128)(2,1)S(1)}, bf16[64,3,8,256]{3,2,1,0:T(8,128)(2,1)}, u32[]{:S(2)}) copy-start(bf16[64,3,8,256]{3,2,1,0:T(8,128)(2,1)} %param.7) | copy-start | bytes 2359300
  67.1 34.0 %copy-start.3 = (f32[64]{0:T(128)S(1)}, f32[64]{0:T(128)}, u32[]{:S(2)}) copy-start(f32[64]{0:T(128)} %param.8) | copy-start | bytes 772
  101.1 0.6 copy-start.2
